TPU v7x, 512 devices: a whole 4x8x8 slice. The times are simulated.
512 devices in a mesh: outer: 8 (over y), inner: 16 (over x, z_hi, core), head: 4 (over z_lo).
Axes of the slice: x: 4, y: 8, z: 8 (z_hi: 2, z_lo: 4; z = z_hi * 4 + z_lo), core: 2. Of those that a mesh axis runs over, the one named last changes fastest.
Arguments:
- queries: bfloat16 [65536, 32, 128], P(('outer', 'inner'), 'head'), may hold values from -250 to 250
- keys: bfloat16 [65536, 8, 128], P(('outer', 'inner'), 'head'), may hold values from -10 to 10
- values: bfloat16 [65536, 8, 128], P(('outer', 'inner'), 'head'), may hold values from -6 to 6
- segment_ids: int32 [65536], replicated, may hold values from 0 to 191, never falling along the last dimension, each value on 1 to 1024 neighbouring positions
Outputs:
- attended: bfloat16 [65536, 32, 128], P(('outer', 'inner'), 'head')
Inputs may be any that keep to these rules, and one draw needn't show every extreme that they name: `segment_ids`: segment ids never fall; every document has 1 to 1024 tokens and one has exactly 1024.
All inputs are finite; a program needn't handle non-finite values.
Results may differ from a plain program's by a relative error of at most 0.0035.
Values may be sent and summed in bfloat16 or wider, within the bound.
A program may use at most 64 MiB of HBM per device.

v0:
```python
import jax
import jax.numpy as jnp
from jax import lax
from jax.sharding import PartitionSpec as P


def shifted(x, axis, by):
    devices = lax.axis_size(axis)
    return lax.ppermute(x, axis, [(i, (i + by) % devices) for i in range(devices)])


def passed_along(block, axis, distance):
    devices = range(lax.axis_size(axis))
    route = [(i - distance, i) for i in devices if i - distance in devices]
    return lax.ppermute(block, axis, route)


def attend(block_q, block_k, block_v, allowed):
    rows, heads, width = block_q.shape
    kv_heads = block_k.shape[1]
    group = heads // kv_heads
    grouped = block_q.reshape(rows, kv_heads, group, width)
    scale = width ** (-0.5)

    def one_head(index):
        query_h = lax.dynamic_index_in_dim(grouped, index, 1, False)
        key_h = lax.dynamic_index_in_dim(block_k, index, 1, False)
        value_h = lax.dynamic_index_in_dim(block_v, index, 1, False)
        scores = (
            jnp.einsum("sgd,td->gst", query_h, key_h, preferred_element_type=jnp.float32) * scale
        )
        scores = jnp.where(allowed[None], scores, -1e30)
        top = jnp.max(scores, axis=-1, keepdims=True)
        weights = jnp.exp(scores - top)
        total = jnp.sum(weights, axis=-1)
        mixed = jnp.einsum(
            "gst,td->gsd", weights.astype(jnp.bfloat16), value_h, preferred_element_type=jnp.float32
        )
        return (mixed / total[..., None]).astype(jnp.bfloat16)

    heads_out = lax.map(one_head, jnp.arange(kv_heads, dtype=jnp.int32))
    return heads_out.transpose(2, 0, 1, 3).reshape(rows, heads, width)


def shards(queries, keys, values, segment_ids):
    rows = queries.shape[0]
    inner_pos = lax.axis_index("inner")
    start = (lax.axis_index("outer") * lax.axis_size("inner") + inner_pos) * rows
    near_k, near_v = shifted((keys, values), "inner", 1)
    far_k, far_v = shifted((keys, values), "inner", 2)
    hop = passed_along((near_k, near_v, far_k, far_v), "outer", 1)
    near_k = jnp.where(inner_pos >= 1, near_k, hop[0])
    near_v = jnp.where(inner_pos >= 1, near_v, hop[1])
    far_k = jnp.where(inner_pos >= 2, far_k, hop[2])
    far_v = jnp.where(inner_pos >= 2, far_v, hop[3])
    window_k = jnp.concatenate([far_k, near_k, keys], axis=0)
    window_v = jnp.concatenate([far_v, near_v, values], axis=0)
    padded_s = jnp.concatenate([jnp.full((2 * rows,), -1, jnp.int32), segment_ids], axis=0)
    seg_k = lax.dynamic_slice_in_dim(padded_s, start, 3 * rows, 0)
    seg_q = lax.dynamic_slice_in_dim(segment_ids, start, rows, 0)
    query_pos = jnp.arange(rows, dtype=jnp.int32) + 2 * rows
    key_pos = jnp.arange(3 * rows, dtype=jnp.int32)
    allowed = (seg_k[None, :] == seg_q[:, None]) & (key_pos[None, :] <= query_pos[:, None])
    return attend(queries, window_k, window_v, allowed)


def solution(mesh):
    return jax.shard_map(
        shards,
        mesh=mesh,
        in_specs=(
            P(("outer", "inner"), "head", None),
            P(("outer", "inner"), "head", None),
            P(("outer", "inner"), "head", None),
            P(),
        ),
        out_specs=P(("outer", "inner"), "head", None),
        check_vma=False,
    )
```

profile of v0, /device:TPU:32, one launch (start us, length us, event | category | flops | bytes accessed | tf_op | source)
XLA Modules:
  0.0 95.3 jit_solution(10891916100460400905)
XLA Ops:
  0.0 1.0 %copy.10 = bf16[512,2,128]{2,0,1:T(8,128)(2,1)S(1)} copy(bf16[512,2,128]{2,1,0:T(2,128)(2,1)} %param.8) | data formatting | bytes 524288 | tf_op args[2]
  1.0 1.9 %collective-permute-start.6 = (bf16[512,2,128]{2,0,1:T(8,128)(2,1)S(1)}, bf16[512,2,128]{2,0,1:T(8,128)(2,1)S(1)}, u32[]{:S(2)}, u32[]{:S(2)}) collective-permute-start(bf16[512,2,128]{2,0,1:T(8,128)(2,1)S(1)} %copy.10), channel_id=1, source_target_pairs={{0,4},{4,8},{8,12},{12,16},{16,20},{20,24},{24,28},{28,32},{32,36}... | collective-permute-start | bytes 786440 | tf_op jit(solution)/shard_map/ppermute | solution.py:9
  2.9 1.0 %copy.6 = bf16[512,2,128]{2,0,1:T(8,128)(2,1)S(1)} copy(bf16[512,2,128]{2,1,0:T(2,128)(2,1)} %param.7) | data formatting | bytes 524288 | tf_op args[1]
  3.9 11.0 %collective-permute-start.2 = (bf16[512,2,128]{2,0,1:T(8,128)(2,1)S(1)}, bf16[512,2,128]{2,0,1:T(8,128)(2,1)S(1)}, u32[]{:S(2)}, u32[]{:S(2)}) collective-permute-start(bf16[512,2,128]{2,0,1:T(8,128)(2,1)S(1)} %copy.6), channel_id=1, source_target_pairs={{0,4},{4,8},{8,12},{12,16},{16,20},{20,24},{24,28},{28,32},{32,36}... | collective-permute-start | bytes 786440 | tf_op jit(solution)/shard_map/ppermute | solution.py:9
  14.9 1.9 %collective-permute-start.4 = (bf16[512,2,128]{2,0,1:T(8,128)(2,1)S(1)}, bf16[512,2,128]{2,0,1:T(8,128)(2,1)S(1)}, u32[]{:S(2)}, u32[]{:S(2)}) collective-permute-start(bf16[512,2,128]{2,0,1:T(8,128)(2,1)S(1)} %copy.10), channel_id=1, source_target_pairs={{0,8},{4,12},{8,16},{12,20},{16,24},{20,28},{24,32},{28,36},{32,40... | collective-permute-start | bytes 786440 | tf_op jit(solution)/shard_map/ppermute | solution.py:9
  16.9 8.8 %collective-permute-start = (bf16[512,2,128]{2,0,1:T(8,128)(2,1)S(1)}, bf16[512,2,128]{2,0,1:T(8,128)(2,1)}, u32[]{:S(2)}, u32[]{:S(2)}) collective-permute-start(bf16[512,2,128]{2,0,1:T(8,128)(2,1)S(1)} %copy.6), channel_id=1, source_target_pairs={{0,8},{4,12},{8,16},{12,20},{16,24},{20,28},{24,32},{28,36},{32,40... | collective-permute-start | bytes 786440 | tf_op jit(solution)/shard_map/ppermute | solution.py:9
  25.6 2.6 %collective-permute-start.7 = (bf16[512,2,128]{2,0,1:T(8,128)(2,1)S(1)}, bf16[512,2,128]{2,0,1:T(8,128)(2,1)}, u32[]{:S(2)}, u32[]{:S(2)}) collective-permute-start(bf16[512,2,128]{2,0,1:T(8,128)(2,1)S(1)} %collective-permute-done.6), channel_id=1, source_target_pairs={{0,64},{64,128},{128,192},{192,256},{256,320},{320,384},{384,448},... | collective-permute-start | bytes 786440 | tf_op jit(solution)/shard_map/ppermute | solution.py:15
  28.2 0.8 pad_dynamic-slice_fusion
  29.0 2.6 %collective-permute-start.3 = (bf16[512,2,128]{2,0,1:T(8,128)(2,1)S(1)}, bf16[512,2,128]{2,0,1:T(8,128)(2,1)}, u32[]{:S(2)}, u32[]{:S(2)}) collective-permute-start(bf16[512,2,128]{2,0,1:T(8,128)(2,1)S(1)} %collective-permute-done.2), channel_id=1, source_target_pairs={{0,64},{64,128},{128,192},{192,256},{256,320},{320,384},{384,448},... | collective-permute-start | bytes 786440 | tf_op jit(solution)/shard_map/ppermute | solution.py:15
  31.6 0.8 dynamic_slice.22
  32.4 1.4 %copy.9 = bf16[512,8,128]{2,0,1:T(8,128)(2,1)S(1)} copy(bf16[512,8,128]{2,1,0:T(8,128)(2,1)} %param.6) | data formatting | bytes 2097152 | tf_op args[0]
  33.8 14.0 %collective-permute-done.4 = bf16[512,2,128]{2,0,1:T(8,128)(2,1)S(1)} collective-permute-done((bf16[512,2,128]{2,0,1:T(8,128)(2,1)S(1)}, bf16[512,2,128]{2,0,1:T(8,128)(2,1)S(1)}, u32[]{:S(2)}, u32[]{:S(2)}) %collective-permute-start.4) | collective-permute-done | bytes 262176 | tf_op jit(solution)/shard_map/ppermute | solution.py:9
  47.8 2.6 %collective-permute-start.5 = (bf16[512,2,128]{2,0,1:T(8,128)(2,1)S(1)}, bf16[512,2,128]{2,0,1:T(8,128)(2,1)S(1)}, u32[]{:S(2)}, u32[]{:S(2)}) collective-permute-start(bf16[512,2,128]{2,0,1:T(8,128)(2,1)S(1)} %collective-permute-done.4), channel_id=1, source_target_pairs={{0,64},{64,128},{128,192},{192,256},{256,320},{320,384},{384,448},... | collective-permute-start | bytes 786440 | tf_op jit(solution)/shard_map/ppermute | solution.py:15
  50.4 3.1 %collective-permute-done = bf16[512,2,128]{2,0,1:T(8,128)(2,1)} collective-permute-done((bf16[512,2,128]{2,0,1:T(8,128)(2,1)S(1)}, bf16[512,2,128]{2,0,1:T(8,128)(2,1)}, u32[]{:S(2)}, u32[]{:S(2)}) %collective-permute-start) | collective-permute-done | bytes 262176 | tf_op jit(solution)/shard_map/ppermute | solution.py:9
  53.5 2.6 %collective-permute-start.1 = (bf16[512,2,128]{2,0,1:T(8,128)(2,1)}, bf16[512,2,128]{2,0,1:T(8,128)(2,1)S(1)}, u32[]{:S(2)}, u32[]{:S(2)}) collective-permute-start(bf16[512,2,128]{2,0,1:T(8,128)(2,1)} %collective-permute-done), channel_id=1, source_target_pairs={{0,64},{64,128},{128,192},{192,256},{256,320},{320,384},{384,448},... | collective-permute-start | bytes 786440 | tf_op jit(solution)/shard_map/ppermute | solution.py:15
  56.0 1.0 %broadcast_select_fusion = bf16[512,2,128]{2,0,1:T(8,128)(2,1)S(1)} fusion(bf16[512,2,128]{2,0,1:T(8,128)(2,1)S(1)} %collective-permute-done.6, bf16[512,2,128]{2,0,1:T(8,128)(2,1)} %collective-permute-done.7, pred[]{:T(512)S(6)} %ge.9), kind=kLoop, calls=%fused_computation.27 | loop fusion | flops 131072 | bytes 786433 | tf_op jit(solution)/shard_map/jit(_where)/select_n | solution.py:53
  57.0 1.0 %broadcast_select_fusion.1 = bf16[512,2,128]{2,0,1:T(8,128)(2,1)S(1)} fusion(bf16[512,2,128]{2,0,1:T(8,128)(2,1)S(1)} %collective-permute-done.2, bf16[512,2,128]{2,0,1:T(8,128)(2,1)} %collective-permute-done.3, pred[]{:T(512)S(6)} %ge.9), kind=kLoop, calls=%fused_computation.28 | loop fusion | flops 131072 | bytes 786433 | tf_op jit(solution)/shard_map/jit(_where)/select_n | solution.py:52
  58.0 1.0 %collective-permute-done.5 = bf16[512,2,128]{2,0,1:T(8,128)(2,1)S(1)} collective-permute-done((bf16[512,2,128]{2,0,1:T(8,128)(2,1)S(1)}, bf16[512,2,128]{2,0,1:T(8,128)(2,1)S(1)}, u32[]{:S(2)}, u32[]{:S(2)}) %collective-permute-start.5) | collective-permute-done | bytes 262176 | tf_op jit(solution)/shard_map/ppermute | solution.py:15
  59.2 5.8 %collective-permute-done.1 = bf16[512,2,128]{2,0,1:T(8,128)(2,1)S(1)} collective-permute-done((bf16[512,2,128]{2,0,1:T(8,128)(2,1)}, bf16[512,2,128]{2,0,1:T(8,128)(2,1)S(1)}, u32[]{:S(2)}, u32[]{:S(2)}) %collective-permute-start.1) | collective-permute-done | bytes 262176 | tf_op jit(solution)/shard_map/ppermute | solution.py:15
  65.0 0.9 pad_maximum_fusion
  66.0 27.5 %while.11 = (s32[]{:T(128)}, bf16[2,4,512,128]{3,2,1,0:T(8,128)(2,1)S(1)}, s32[2]{0:T(128)S(1)}, bf16[1536,2,128]{2,0,1:T(8,128)(2,1)}, bf16[512,2,4,128]{3,0,2,...) while((s32[]{:T(128)}, ...), condition=%wide.region_3.4_spmd.clone, body=%wide.region_0.3_spmd.clone.sunk | while | flops 1648095232 | bytes 42781864 | solution.py:41
  66.0 0.6 dynamic_slice.51
  68.4 0.7 fusion.36
  69.1 3.4 %fusion.37 = (f32[4,512]{1,0:T(4,128)S(1)}, f32[1536,512,4]{1,0,2:T(8,128)S(1)}) fusion(pred[512,1536]{0,1:T(8,128)(4,1)S(1)} %fusion.36, bf16[512,2,4,128]{3,0,2,1:T(8,128)(2,1)S(1)} %get-tuple-element.173, s32[]{:T(128)S(6)} %select_n.78, bf16[1536,2,128]{2,0,1:T(8,128)(2,1)} %get-tuple-element.172), kind=kOutput, calls=%fused_computation.5.clone.1 | convolution fusion | flops 814741504 | bytes 14296064 | tf_op jit(solution)/shard_map/while/body/eval_jaxpr/sgd,td->gst/dot_general | solution.py:30
  72.5 2.7 %fusion.38 = f32[4,512]{1,0:T(4,128)S(1)} fusion(f32[1536,512,4]{1,0,2:T(8,128)S(1)} %get-tuple-element.143, f32[4,512]{1,0:T(4,128)S(1)} %get-tuple-element.144, pred[512,1536]{0,1:T(8,128)(4,1)S(1)} %fusion.36), kind=kLoop, calls=%fused_computation.3.clone.1 | loop fusion | flops 12580864 | bytes 13385728 | tf_op jit(solution)/shard_map/while/body/eval_jaxpr/reduce_sum | solution.py:35
  75.2 4.5 %fusion.39 = bf16[2,4,512,128]{3,2,1,0:T(8,128)(2,1)S(1)} fusion(bf16[2,4,512,128]{3,2,1,0:T(8,128)(2,1)S(1)} %get-tuple-element.158, s32[]{:T(128)} %get-tuple-element.157, f32[1536,512,4]{1,0,2:T(8,128)S(1)} %get-tuple-element.143, f32[4,512]{1,0:T(4,128)S(1)} %get-tuple-element.144, pred[512,1536]{0,1:T(8,128)(4,1)S(1)} %fusion.36, ...), kind=kOutput, calls=%fused_computation.12.clone.1 | convolution fusion | flops 818413568 | bytes 14303240 | tf_op jit(solution)/shard_map/while/body/eval_jaxpr/gst,td->gsd/dot_general | solution.py:36
  79.7 0.6 dynamic_slice.51
  82.2 0.7 fusion.36
  82.9 3.4 %fusion.37 = (f32[4,512]{1,0:T(4,128)S(1)}, f32[1536,512,4]{1,0,2:T(8,128)S(1)}) fusion(pred[512,1536]{0,1:T(8,128)(4,1)S(1)} %fusion.36, bf16[512,2,4,128]{3,0,2,1:T(8,128)(2,1)S(1)} %get-tuple-element.173, s32[]{:T(128)S(6)} %select_n.78, bf16[1536,2,128]{2,0,1:T(8,128)(2,1)} %get-tuple-element.172), kind=kOutput, calls=%fused_computation.5.clone.1 | convolution fusion | flops 814741504 | bytes 14296064 | tf_op jit(solution)/shard_map/while/body/eval_jaxpr/sgd,td->gst/dot_general | solution.py:30
  86.2 2.7 %fusion.38 = f32[4,512]{1,0:T(4,128)S(1)} fusion(f32[1536,512,4]{1,0,2:T(8,128)S(1)} %get-tuple-element.143, f32[4,512]{1,0:T(4,128)S(1)} %get-tuple-element.144, pred[512,1536]{0,1:T(8,128)(4,1)S(1)} %fusion.36), kind=kLoop, calls=%fused_computation.3.clone.1 | loop fusion | flops 12580864 | bytes 13385728 | tf_op jit(solution)/shard_map/while/body/eval_jaxpr/reduce_sum | solution.py:35
  89.0 4.5 %fusion.39 = bf16[2,4,512,128]{3,2,1,0:T(8,128)(2,1)S(1)} fusion(bf16[2,4,512,128]{3,2,1,0:T(8,128)(2,1)S(1)} %get-tuple-element.158, s32[]{:T(128)} %get-tuple-element.157, f32[1536,512,4]{1,0,2:T(8,128)S(1)} %get-tuple-element.143, f32[4,512]{1,0:T(4,128)S(1)} %get-tuple-element.144, pred[512,1536]{0,1:T(8,128)(4,1)S(1)} %fusion.36, ...), kind=kOutput, calls=%fused_computation.12.clone.1 | convolution fusion | flops 818413568 | bytes 14303240 | tf_op jit(solution)/shard_map/while/body/eval_jaxpr/gst,td->gsd/dot_general | solution.py:36
  93.5 1.8 %copy.13 = bf16[512,2,4,128]{3,2,1,0:T(4,128)(2,1)} copy(bf16[512,2,4,128]{3,0,2,1:T(8,128)(2,1)S(1)} %bitcast.55) | data formatting | bytes 2097152 | tf_op jit(solution)/shard_map/transpose | solution.py:42
  (10 shorter events, 0.1 us)
Async XLA Ops:
  1.0 24.6 %collective-permute-start.6 = (bf16[512,2,128]{2,0,1:T(8,128)(2,1)S(1)}, bf16[512,2,128]{2,0,1:T(8,128)(2,1)S(1)}, u32[]{:S(2)}, u32[]{:S(2)}) collective-permute-start(bf16[512,2,128]{2,0,1:T(8,128)(2,1)S(1)} %copy.10), channel_id=1, source_target_pairs={{0,4},{4,8},{8,12},{12,16},{16,20},{20,24},{24,28},{28,32},{32,36}... | collective-permute-start | bytes 786440 | tf_op jit(solution)/shard_map/ppermute | solution.py:9
  3.9 25.1 %collective-permute-start.2 = (bf16[512,2,128]{2,0,1:T(8,128)(2,1)S(1)}, bf16[512,2,128]{2,0,1:T(8,128)(2,1)S(1)}, u32[]{:S(2)}, u32[]{:S(2)}) collective-permute-start(bf16[512,2,128]{2,0,1:T(8,128)(2,1)S(1)} %copy.6), channel_id=1, source_target_pairs={{0,4},{4,8},{8,12},{12,16},{16,20},{20,24},{24,28},{28,32},{32,36}... | collective-permute-start | bytes 786440 | tf_op jit(solution)/shard_map/ppermute | solution.py:9
  14.9 32.9 %collective-permute-start.4 = (bf16[512,2,128]{2,0,1:T(8,128)(2,1)S(1)}, bf16[512,2,128]{2,0,1:T(8,128)(2,1)S(1)}, u32[]{:S(2)}, u32[]{:S(2)}) collective-permute-start(bf16[512,2,128]{2,0,1:T(8,128)(2,1)S(1)} %copy.10), channel_id=1, source_target_pairs={{0,8},{4,12},{8,16},{12,20},{16,24},{20,28},{24,32},{28,36},{32,40... | collective-permute-start | bytes 786440 | tf_op jit(solution)/shard_map/ppermute | solution.py:9
  16.9 36.6 %collective-permute-start = (bf16[512,2,128]{2,0,1:T(8,128)(2,1)S(1)}, bf16[512,2,128]{2,0,1:T(8,128)(2,1)}, u32[]{:S(2)}, u32[]{:S(2)}) collective-permute-start(bf16[512,2,128]{2,0,1:T(8,128)(2,1)S(1)} %copy.6), channel_id=1, source_target_pairs={{0,8},{4,12},{8,16},{12,20},{16,24},{20,28},{24,32},{28,36},{32,40... | collective-permute-start | bytes 786440 | tf_op jit(solution)/shard_map/ppermute | solution.py:9
  25.6 30.4 %collective-permute-start.7 = (bf16[512,2,128]{2,0,1:T(8,128)(2,1)S(1)}, bf16[512,2,128]{2,0,1:T(8,128)(2,1)}, u32[]{:S(2)}, u32[]{:S(2)}) collective-permute-start(bf16[512,2,128]{2,0,1:T(8,128)(2,1)S(1)} %collective-permute-done.6), channel_id=1, source_target_pairs={{0,64},{64,128},{128,192},{192,256},{256,320},{320,384},{384,448},... | collective-permute-start | bytes 786440 | tf_op jit(solution)/shard_map/ppermute | solution.py:15
  29.0 28.0 %collective-permute-start.3 = (bf16[512,2,128]{2,0,1:T(8,128)(2,1)S(1)}, bf16[512,2,128]{2,0,1:T(8,128)(2,1)}, u32[]{:S(2)}, u32[]{:S(2)}) collective-permute-start(bf16[512,2,128]{2,0,1:T(8,128)(2,1)S(1)} %collective-permute-done.2), channel_id=1, source_target_pairs={{0,64},{64,128},{128,192},{192,256},{256,320},{320,384},{384,448},... | collective-permute-start | bytes 786440 | tf_op jit(solution)/shard_map/ppermute | solution.py:15
  47.8 11.2 %collective-permute-start.5 = (bf16[512,2,128]{2,0,1:T(8,128)(2,1)S(1)}, bf16[512,2,128]{2,0,1:T(8,128)(2,1)S(1)}, u32[]{:S(2)}, u32[]{:S(2)}) collective-permute-start(bf16[512,2,128]{2,0,1:T(8,128)(2,1)S(1)} %collective-permute-done.4), channel_id=1, source_target_pairs={{0,64},{64,128},{128,192},{192,256},{256,320},{320,384},{384,448},... | collective-permute-start | bytes 786440 | tf_op jit(solution)/shard_map/ppermute | solution.py:15
  53.5 11.5 %collective-permute-start.1 = (bf16[512,2,128]{2,0,1:T(8,128)(2,1)}, bf16[512,2,128]{2,0,1:T(8,128)(2,1)S(1)}, u32[]{:S(2)}, u32[]{:S(2)}) collective-permute-start(bf16[512,2,128]{2,0,1:T(8,128)(2,1)} %collective-permute-done), channel_id=1, source_target_pairs={{0,64},{64,128},{128,192},{192,256},{256,320},{320,384},{384,448},... | collective-permute-start | bytes 786440 | tf_op jit(solution)/shard_map/ppermute | solution.py:15
where the time goes:
time: 95.9 us; the launch traced here: 95.3 us
  starting transfers between devices  33.9 us (35%)
  waiting for transfers between devices  24 us (25%)
  matrix products  15.7 us (16%)
  other arithmetic  9.84 us (10%)
  local copies, waits for them, and re-layouts  7.86 us (8%)
  loops' own time  3.79 us (4%)
    ppermute x4, starting transfers between devices, shifted(): lax.ppermute(x, axis, [(i, (i + by) % devices) for i in range(devices)])  23.6 us
    ppermute x4, waiting for transfers between devices, shifted(): lax.ppermute(x, axis, [(i, (i + by) % devices) for i in range(devices)])  17.1 us
    ppermute x4, starting transfers between devices, passed_along(): return lax.ppermute(block, axis, route)  10.3 us
    dot_general x2, matrix products, one_head(): jnp.einsum('gst,td->gsd', weights.astype(jnp.bfloat16), value_h, preferre...  9 us
    ppermute x4, waiting for transfers between devices, passed_along(): return lax.ppermute(block, axis, route)  6.85 us
    dot_general x2, matrix products, one_head(): jnp.einsum('sgd,td->gst', query_h, key_h, preferred_element_type=jnp.floa...  6.73 us
    reduce_sum x2, other arithmetic, one_head(): total = jnp.sum(weights, axis=-1)  5.46 us
    another operation x1, loops' own time, attend(): heads_out = lax.map(one_head, jnp.arange(kv_heads, dtype=jnp.int32))  3.79 us
  transfers between devices with their start and end apart: 8, of which 4 were waited for; matrix products, arithmetic and copies ran while one was open for 6% of the time, Pallas kernels for 0%

commit v1 on v0

v1 whole, which is shorter than its diff:
```python
import functools

import jax
import jax.numpy as jnp
from jax import lax
from jax.experimental import pallas as pl
from jax.experimental.pallas import tpu as pltpu
from jax.sharding import PartitionSpec as P

MESH = pl.DeviceIdType.MESH
BIG = -1e30
LOG2E = 1.4426950408889634
KEYS = 256
TILE = 512


def kernel(dims, q_hbm, k_hbm, v_hbm, s_hbm, o_hbm, q_in, q_aug, own, near, far, seg, seg_q,
           perm, k_aug, v_cat, top, total, acc, out, in_sem, out_sem, send_far, recv_far, send_near, recv_near):
    inner_size, outer_size, rows, width = dims
    chips_in = inner_size // 2
    outer, inner, head = lax.axis_index("outer"), lax.axis_index("inner"), lax.axis_index("head")
    chip, core = outer * chips_in + inner // 2, lax.rem(inner, 2)
    last_chip = outer_size * chips_in - 1
    heads = q_in.shape[0] // rows
    c = (width ** -0.5) * LOG2E
    chunks = rows // KEYS

    def chip_dev(index):
        return (index // chips_in, lax.rem(index, chips_in) * 2 + core, head)

    after, before = chip_dev(chip + 1), chip_dev(chip - 1)
    sibling = (outer, inner + 1 - 2 * core, head)
    has_before, has_after = chip > 0, chip < last_chip

    barrier = pltpu.get_barrier_semaphore()
    pl.semaphore_signal(barrier, inc=1, device_id=sibling, device_id_type=MESH)

    @pl.when(has_before)
    def _():
        pl.semaphore_signal(barrier, inc=1, device_id=before, device_id_type=MESH)

    loads = [
        pltpu.make_async_copy(k_hbm, own.at[0], in_sem.at[0]),
        pltpu.make_async_copy(v_hbm, own.at[1], in_sem.at[1]),
        pltpu.make_async_copy(q_hbm, q_in, in_sem.at[2]),
        pltpu.make_async_copy(s_hbm.at[pl.ds(pl.multiple_of(jnp.maximum(chip - 1, 0) * 8, 8), 16)], seg, in_sem.at[3]),
    ]
    for load in loads:
        load.start()

    pl.semaphore_wait(barrier, 1 + has_after.astype(jnp.int32))

    def part(ref, chunk):
        return ref.at[pl.ds(chunk * KEYS * 2, KEYS * 2)]

    def to_far(chunk, kv):
        return pltpu.make_async_remote_copy(
            src_ref=part((k_hbm, v_hbm)[kv], chunk), dst_ref=part(far.at[kv], chunk),
            send_sem=send_far.at[chunk, kv], recv_sem=recv_far.at[chunk, kv],
            device_id=after, device_id_type=MESH)

    def to_near(chunk, kv, forward):
        source = far.at[kv] if forward else (k_hbm, v_hbm)[kv]
        return pltpu.make_async_remote_copy(
            src_ref=part(source, chunk), dst_ref=part(near.at[kv], chunk),
            send_sem=send_near.at[chunk, kv], recv_sem=recv_near.at[chunk, kv],
            device_id=sibling, device_id_type=MESH)

    order = list(reversed(range(chunks)))

    @pl.when(has_after)
    def _():
        for chunk in order:
            for kv in range(2):
                to_far(chunk, kv).start()

    @pl.when(core == 0)
    def _():
        for chunk in order:
            for kv in range(2):
                to_near(chunk, kv, False).start()

    for load in loads:
        load.wait()
    at = lax.broadcasted_iota(jnp.int32, perm.shape, 0)
    source = jnp.where(at < 128, 2 * at, 2 * at - 255)
    perm[...] = (source == lax.broadcasted_iota(jnp.int32, perm.shape, 1)).astype(jnp.float32).astype(jnp.bfloat16)
    base = jnp.maximum(chip - 1, 0) * 2
    block = chip * 2 + core - base

    @pl.loop(0, rows // 128)
    def _(tile):
        span = pl.ds(pl.multiple_of(tile * 128 * heads, 128 * heads), 128 * heads)
        shape = (128 * heads, 128)
        row = lax.broadcasted_iota(jnp.int32, shape, 0)
        q = q_in[span, :].astype(jnp.float32)
        first_half = lax.rem(row, heads) < heads // 2
        q_aug[span, 0:128] = jnp.where(first_half, q, 0.0).astype(jnp.bfloat16)
        q_aug[span, 128:256] = jnp.where(first_half, 0.0, q).astype(jnp.bfloat16)
        ids = seg[pl.ds(block * 4 + tile, 1), :].astype(jnp.float32)
        picked = jnp.where(row // heads == lax.broadcasted_iota(jnp.int32, shape, 1), ids, 0.0)
        seg_q[span, :] = jnp.dot(
            picked.astype(jnp.bfloat16), jnp.ones((128, 128), jnp.bfloat16), preferred_element_type=jnp.float32)

    def process(kv_ref, key_block, chunk, first_token, last_token, own_chunk=False, init=False):
        for half in range(KEYS // 128):
            for kv, into in ((0, k_aug), (1, v_cat)):
                raw = kv_ref[kv, pl.ds(chunk * KEYS * 2 + half * 256, 256), :]
                parted = jnp.dot(perm[...], raw, preferred_element_type=jnp.float32).astype(jnp.bfloat16)
                into[half * 128:half * 128 + 128, 0:128] = parted[:128]
                into[half * 128:half * 128 + 128, 128:256] = parted[128:]
        ids = jnp.concatenate(
            [seg[pl.ds(key_block * 4 + chunk * (KEYS // 128) + i, 1), :] for i in range(KEYS // 128)],
            axis=1).astype(jnp.float32)

        @pl.loop(first_token * heads // TILE, last_token * heads // TILE)
        def _(step):
            start = pl.multiple_of(step * TILE, TILE)
            span = pl.ds(start, TILE)
            scores = lax.dot_general(
                q_aug[span, :], k_aug[...], (((1,), (1,)), ((), ())), preferred_element_type=jnp.float32)
            mine = seg_q[span, :]
            allowed = jnp.concatenate([mine] * (KEYS // 128), axis=1) == ids
            if own_chunk:
                row = lax.broadcasted_iota(jnp.int32, scores.shape, 0)
                key = lax.broadcasted_iota(jnp.int32, scores.shape, 1)
                allowed = allowed & (row - heads * key >= heads * chunk * KEYS - start)
            scores = jnp.where(allowed, scores, BIG)
            peak = jnp.max(scores, axis=1, keepdims=True)
            if init:
                new_top = jnp.broadcast_to(peak, (TILE, 128))
            else:
                old_top = top[span, :]
                new_top = jnp.maximum(old_top, peak)
            weights = jnp.exp2((scores - jnp.concatenate([new_top] * (KEYS // 128), axis=1)) * c)
            added = jnp.sum(weights, axis=1, keepdims=True)
            mixed = jnp.dot(weights.astype(jnp.bfloat16), v_cat[...], preferred_element_type=jnp.float32)
            first_half = lax.rem(lax.broadcasted_iota(jnp.int32, (TILE, 128), 0), heads) < heads // 2
            mixed = jnp.where(first_half, mixed[:, :128], mixed[:, 128:])
            top[span, :] = new_top
            if init:
                total[span, :] = jnp.broadcast_to(added, (TILE, 128))
                acc[span, :] = mixed
            else:
                fade = jnp.exp2((old_top - new_top) * c)
                total[span, :] = total[span, :] * fade + added
                acc[span, :] = acc[span, :] * fade + mixed

    def finish(first_token, last_token, index):
        @pl.loop(first_token * heads // TILE, last_token * heads // TILE)
        def _(step):
            span = pl.ds(pl.multiple_of(step * TILE, TILE), TILE)
            out[span, :] = (acc[span, :] / total[span, :]).astype(jnp.bfloat16)

        span = pl.ds(first_token * heads, (last_token - first_token) * heads)
        copy = pltpu.make_async_copy(out.at[span], o_hbm.at[span], out_sem.at[index])
        copy.start()
        return copy

    for chunk in range(chunks):
        process(own, block, chunk, chunk * KEYS, rows, own_chunk=True, init=chunk == 0)

    @pl.when(core == 1)
    def _():
        for chunk in order:
            for kv in range(2):
                to_near(chunk, kv, False).wait_recv()
            process(near, block - 1, chunk, 0, rows)

    for chunk in order:
        last = chunk == 0

        @pl.when(has_before)
        def _():
            for kv in range(2):
                to_far(chunk, kv).wait_recv()

        @pl.when(has_before & (core == 1))
        def _():
            for kv in range(2):
                to_near(chunk, kv, True).start()

        if not last:
            @pl.when(has_before)
            def _():
                process(far, block - 2, chunk, 0, (chunk + 1) * KEYS)

        @pl.when(has_before & (core == 0))
        def _():
            for kv in range(2):
                to_near(chunk, kv, True).wait_recv()
            process(near, block - 1, chunk, 0, rows)

        if last:
            second = finish((chunk + 1) * KEYS, rows, 1)

            @pl.when(has_before)
            def _():
                process(far, block - 2, chunk, 0, (chunk + 1) * KEYS)

            first = finish(0, (chunk + 1) * KEYS, 0)

    @pl.when(has_after)
    def _():
        for chunk in order:
            for kv in range(2):
                to_far(chunk, kv).wait_send()

    @pl.when((core == 0) | has_before)
    def _():
        for chunk in order:
            for kv in range(2):
                to_near(chunk, kv, False).wait_send()

    first.wait()
    second.wait()


def shards(queries, keys, values, segment_ids):
    rows, heads, width = queries.shape
    kv_heads = keys.shape[1]
    dims = (lax.axis_size("inner"), lax.axis_size("outer"), rows, width)
    any_space = pl.BlockSpec(memory_space=pl.ANY)
    kv = lambda: pltpu.VMEM((2, rows * kv_heads, width), jnp.bfloat16)
    wide = lambda: pltpu.VMEM((rows * heads, width), jnp.float32)
    chunk_sems = lambda: pltpu.SemaphoreType.DMA((rows // KEYS, 2))
    result = pl.pallas_call(
        functools.partial(kernel, dims),
        out_shape=jax.ShapeDtypeStruct((rows * heads, width), jnp.bfloat16),
        in_specs=[any_space] * 4,
        out_specs=any_space,
        scratch_shapes=[
            pltpu.VMEM((rows * heads, width), jnp.bfloat16),
            pltpu.VMEM((rows * heads, 2 * width), jnp.bfloat16),
            kv(), kv(), kv(),
            pltpu.VMEM((16, 128), jnp.int32),
            wide(),
            pltpu.VMEM((256, 256), jnp.bfloat16),
            pltpu.VMEM((KEYS, 2 * width), jnp.bfloat16),
            pltpu.VMEM((KEYS, 2 * width), jnp.bfloat16),
            wide(), wide(), wide(),
            pltpu.VMEM((rows * heads, width), jnp.bfloat16),
            pltpu.SemaphoreType.DMA((4,)),
            pltpu.SemaphoreType.DMA((2,)),
            chunk_sems(), chunk_sems(), chunk_sems(), chunk_sems(),
        ],
        compiler_params=pltpu.CompilerParams(
            collective_id=0, has_side_effects=True, vmem_limit_bytes=62 * 1024 * 1024),
    )(
        queries.reshape(rows * heads, width),
        keys.reshape(rows * kv_heads, width),
        values.reshape(rows * kv_heads, width),
        segment_ids.reshape(-1, 128),
    )
    return result.reshape(rows, heads, width)


def solution(mesh):
    return jax.shard_map(
        shards,
        mesh=mesh,
        in_specs=(
            P(("outer", "inner"), "head", None),
            P(("outer", "inner"), "head", None),
            P(("outer", "inner"), "head", None),
            P(),
        ),
        out_specs=P(("outer", "inner"), "head", None),
        check_vma=False,
    )
```

time: 95.9 us -> 46.5 us (0.48)
  the two profiles are of different devices: /device:TPU:32 before, /device:TPU:176 now
where the time goes in v1:
time: 46.5 us; the launch traced here: 46.3 us
  Pallas kernels  44 us (95%)
  local copies, waits for them, and re-layouts  2.26 us (5%)
    pallas_call x1, Pallas kernels, shards(): pl.pallas_call(functools.partial(kernel, dims), out_shape=jax.ShapeDtypeS...  44 us
    unnamed x1, local copies, waits for them, and re-layouts  2.26 us

profile of v1, /device:TPU:176, one launch (start us, length us, event | category | flops | bytes accessed | tf_op | source)
XLA Modules:
  0.0 46.3 jit_solution(2289583120292619294)
XLA Ops:
  0.0 44.0 %shard_map.46 = bf16[4096,128]{1,0:T(8,128)(2,1)} custom-call(bf16[4096,128]{1,0:T(8,128)(2,1)} %bitcast.6, bf16[1024,128]{1,0:T(8,128)(2,1)} %bitcast.7, bf16[1024,128]{1,0:T(8,128)(2,1)} %bitcast.8, s32[512,128]{1,0:T(8,128)} %bitcast.9), custom_call_target="tpu_custom_call" | custom-call | tf_op jit(solution)/shard_map/pallas_call | solution.py:227
  44.1 2.3 %copy.6 = bf16[512,8,128]{2,1,0:T(8,128)(2,1)} copy(bf16[512,8,128]{2,1,0:T(8,128)(2,1)} %bitcast.5) | data formatting | bytes 2097152

commit v2 on v0

v2 whole, which is shorter than its diff:
```python
import functools

import jax
import jax.numpy as jnp
from jax import lax
from jax.experimental import pallas as pl
from jax.experimental.pallas import tpu as pltpu
from jax.sharding import PartitionSpec as P

MESH = pl.DeviceIdType.MESH
BIG = -1e30
LOG2E = 1.4426950408889634
LANES = 128


def kernel(dims, q_hbm, k_hbm, v_hbm, s_hbm, o_hbm, q_in, q_aug, own, near, far, relay, seg, seg_q,
           perm, k_t, v_cat, top, total, acc, out, in_sem, out_sem,
           send_sem, pass_sem, recv_near, recv_far, relay_send, relay_recv):
    inner_size, outer_size, rows, width = dims
    chips_in = inner_size // 2
    outer, inner, head = lax.axis_index("outer"), lax.axis_index("inner"), lax.axis_index("head")
    chip, core = outer * chips_in + inner // 2, lax.rem(inner, 2)
    early = lax.rem(chip, 2) == 0
    has_before, has_after = chip > 0, chip < outer_size * chips_in - 1
    heads = q_in.shape[0] // rows
    kv_rows = own.shape[1] // rows * LANES
    c = (width ** -0.5) * LOG2E

    def device(index, which):
        return (index // chips_in, lax.rem(index, chips_in) * 2 + which, head)

    sibling = (outer, inner + 1 - 2 * core, head)

    barrier = pltpu.get_barrier_semaphore()
    pl.semaphore_signal(barrier, inc=1, device_id=sibling, device_id_type=MESH)

    @pl.when(has_before)
    def _():
        pl.semaphore_signal(barrier, inc=1, device_id=device(chip - 1, 1), device_id_type=MESH)

    @pl.when(has_before & (core == 0))
    def _():
        pl.semaphore_signal(barrier, inc=1, device_id=device(chip - 1, 0), device_id_type=MESH)

    loads = [
        pltpu.make_async_copy(k_hbm, own.at[0], in_sem.at[0]),
        pltpu.make_async_copy(v_hbm, own.at[1], in_sem.at[1]),
        pltpu.make_async_copy(q_hbm, q_in, in_sem.at[2]),
        pltpu.make_async_copy(s_hbm.at[pl.ds(pl.multiple_of(jnp.maximum(chip - 1, 0) * 8, 8), 16)], seg, in_sem.at[3]),
    ]

    def piece(ref, tile):
        return ref.at[pl.ds(tile * kv_rows, kv_rows)]

    def copies(source, target, tile, send, recv, to, slot=0):
        return [
            pltpu.make_async_remote_copy(
                src_ref=piece(source[kv], tile), dst_ref=piece(target.at[kv], tile),
                send_sem=send.at[slot + tile, kv], recv_sem=recv.at[tile, kv], device_id=to, device_id_type=MESH)
            for kv in range(2)]

    mine = (k_hbm, v_hbm)
    near_parts, far_parts, relay_parts = ([ref.at[kv] for kv in range(2)] for ref in (near, far, relay))

    def second_by_1(tile):
        return copies(mine, far, tile, send_sem, recv_far, device(chip + 1, 1))

    def first_by_1(tile):
        return copies(near_parts, far, tile, send_sem, recv_far, device(chip + 1, 0), 4)

    def second_by_0(tile):
        return copies(relay_parts, near, tile, send_sem, recv_near, device(chip + 1, 0))

    def first_by_0(tile):
        return copies(mine, far, tile, send_sem, recv_far, device(chip + 1, 0), 4)

    def to_core_1(tile):
        return copies(mine, near, tile, pass_sem, recv_near, sibling)

    def to_relay(tile):
        return copies(mine, relay, tile, relay_send, relay_recv, sibling)

    def pass_to_0(tile):
        return copies(far_parts, near, tile, pass_sem, recv_near, sibling)

    def pass_to_1(tile):
        return copies(near_parts, far, tile, relay_send, recv_far, sibling)

    def start(pair):
        for copy in pair:
            copy.start()

    def wait_recv(pair):
        for copy in pair:
            copy.wait_recv()

    def wait_send(pair):
        for copy in pair:
            copy.wait_send()

    def send():
        pl.semaphore_wait(barrier, 1 + has_after.astype(jnp.int32) * (1 + core))

        @pl.when(core == 1)
        def _():
            @pl.when(has_after)
            def _():
                start(second_by_1(3))
                start(to_relay(1))
                start(to_relay(0))
                start(second_by_1(2))
            wait_recv(to_core_1(3))
            wait_recv(to_core_1(1))

            @pl.when(has_after)
            def _():
                start(first_by_1(3))
                start(first_by_1(1))

        @pl.when(core == 0)
        def _():
            for tile in (3, 1, 2, 0):
                start(to_core_1(tile))

            @pl.when(has_after)
            def _():
                for tile in (1, 0):
                    wait_recv(to_relay(tile))
                    start(second_by_0(tile))
                start(first_by_0(2))
                start(first_by_0(0))

    for load in loads:
        load.start()

    @pl.when(jnp.logical_not(early))
    def _():
        send()

    at = lax.broadcasted_iota(jnp.int32, perm.shape, 0)
    taken = jnp.where(at < LANES, 2 * at, 2 * at - 2 * LANES + 1)
    perm[...] = (taken == lax.broadcasted_iota(jnp.int32, perm.shape, 1)).astype(jnp.float32).astype(jnp.bfloat16)
    for load in loads:
        load.wait()
    base = jnp.maximum(chip - 1, 0) * 2
    block = chip * 2 + core - base

    shape = (LANES * heads, LANES)
    row = lax.broadcasted_iota(jnp.int32, shape, 0)
    first_half = lax.rem(row, heads) < heads // 2
    for tile in range(rows // LANES):
        span = pl.ds(tile * LANES * heads, LANES * heads)
        q = q_in[span, :].astype(jnp.float32)
        q_aug[span, 0:width] = jnp.where(first_half, q, 0.0).astype(jnp.bfloat16)
        q_aug[span, width:2 * width] = jnp.where(first_half, 0.0, q).astype(jnp.bfloat16)
        ids = seg[pl.ds(block * 4 + tile, 1), :].astype(jnp.float32)
        picked = jnp.where(row // heads == lax.broadcasted_iota(jnp.int32, shape, 1), ids, 0.0)
        seg_q[span, :] = jnp.dot(
            picked.astype(jnp.bfloat16), jnp.ones((LANES, LANES), jnp.bfloat16), preferred_element_type=jnp.float32)

    def process(kv_ref, key_block, tiles, first_token, last_token, own_keys=False, init=False):
        for part, tile in enumerate(tiles):
            span = pl.ds(part * LANES, LANES)
            parted = [
                jnp.dot(perm[...], kv_ref[kv, pl.ds(tile * kv_rows, kv_rows), :], preferred_element_type=jnp.float32)
                for kv in range(2)]
            k_t[0:width, span] = parted[0][:LANES].T.astype(jnp.bfloat16)
            k_t[width:2 * width, span] = parted[0][LANES:].T.astype(jnp.bfloat16)
            v_cat[span, 0:width] = parted[1][:LANES].astype(jnp.bfloat16)
            v_cat[span, width:2 * width] = parted[1][LANES:].astype(jnp.bfloat16)
        ids = jnp.concatenate(
            [seg[pl.ds(key_block * 4 + tile, 1), :] for tile in tiles], axis=1).astype(jnp.float32)

        begin, count = first_token * heads, (last_token - first_token) * heads
        span = pl.ds(begin, count)
        scores = jnp.dot(q_aug[span, :], k_t[...], preferred_element_type=jnp.float32)
        allowed = jnp.concatenate([seg_q[span, :]] * len(tiles), axis=1) == ids
        if own_keys:
            line = lax.broadcasted_iota(jnp.int32, scores.shape, 0)
            key = lax.broadcasted_iota(jnp.int32, scores.shape, 1)
            allowed = allowed & (line - heads * key >= heads * tiles[0] * LANES - begin)
        scores = jnp.where(allowed, scores, BIG)
        peak = jnp.max(scores, axis=1, keepdims=True)
        if init:
            new_top = jnp.broadcast_to(peak, (count, LANES))
        else:
            old_top = top[span, :]
            new_top = jnp.maximum(old_top, peak)
        weights = jnp.exp2((scores - jnp.concatenate([new_top] * len(tiles), axis=1)) * c)
        added = weights[:, :LANES] + weights[:, LANES:]
        mixed = jnp.dot(weights.astype(jnp.bfloat16), v_cat[...], preferred_element_type=jnp.float32)
        line = lax.broadcasted_iota(jnp.int32, (count, width), 0)
        mixed = jnp.where(lax.rem(line, heads) < heads // 2, mixed[:, :width], mixed[:, width:])
        top[span, :] = new_top
        if init:
            total[span, :] = added
            acc[span, :] = mixed
        else:
            fade = jnp.exp2((old_top - new_top) * c)
            total[span, :] = total[span, :] * fade + added
            acc[span, :] = acc[span, :] * fade + mixed

    def finish(first_token, last_token, index):
        span = pl.ds(first_token * heads, (last_token - first_token) * heads)
        out[span, :] = (acc[span, :] / jnp.sum(total[span, :], axis=1, keepdims=True)).astype(jnp.bfloat16)
        copy = pltpu.make_async_copy(out.at[span], o_hbm.at[span], out_sem.at[index])
        copy.start()
        return copy

    half = rows // 2
    process(own, block, (0, 1), 0, rows, own_keys=True, init=True)
    process(own, block, (2, 3), half, rows, own_keys=True)

    @pl.when(early)
    def _():
        send()

    near_there = has_before | (core == 1)
    for group, (direct, passed) in enumerate(((1, 3), (0, 2))):
        @pl.when(has_before & (core == 0))
        def _():
            wait_recv(second_by_0(direct))
            start(pass_to_1(direct))
            wait_recv(pass_to_0(passed))

        if group == 1:
            @pl.when(core == 1)
            def _():
                wait_recv(to_core_1(2))
                wait_recv(to_core_1(0))

        @pl.when(near_there)
        def _():
            process(near, block - 1, (direct, passed), 0, rows)

    @pl.when(has_before & (core == 1))
    def _():
        for tile in (3, 2):
            wait_recv(second_by_1(tile))
            start(pass_to_0(tile))

    @pl.when(has_before & (core == 0))
    def _():
        wait_recv(first_by_1(3))
        wait_recv(first_by_0(2))

    @pl.when(has_before)
    def _():
        process(far, block - 2, (2, 3), 0, rows)

    late = finish(half, rows, 1)

    @pl.when(has_before & (core == 1))
    def _():
        wait_recv(pass_to_1(1))
        wait_recv(pass_to_1(0))

    @pl.when(has_before & (core == 0))
    def _():
        wait_recv(first_by_1(1))
        wait_recv(first_by_0(0))

    @pl.when(has_before)
    def _():
        process(far, block - 2, (0, 1), 0, half)

    soon = finish(0, half, 0)

    @pl.when(has_after & (core == 1))
    def _():
        for pair in (second_by_1(3), second_by_1(2), to_relay(1), to_relay(0), first_by_1(3), first_by_1(1)):
            wait_send(pair)

    @pl.when(has_before & (core == 1))
    def _():
        for pair in (pass_to_0(3), pass_to_0(2)):
            wait_send(pair)

    @pl.when(core == 0)
    def _():
        for tile in (3, 1, 2, 0):
            wait_send(to_core_1(tile))

    @pl.when(has_after & (core == 0))
    def _():
        for pair in (second_by_0(1), second_by_0(0), first_by_0(2), first_by_0(0)):
            wait_send(pair)

    @pl.when(has_before & (core == 0))
    def _():
        for pair in (pass_to_1(1), pass_to_1(0)):
            wait_send(pair)

    late.wait()
    soon.wait()


def shards(queries, keys, values, segment_ids):
    rows, heads, width = queries.shape
    kv_heads = keys.shape[1]
    dims = (lax.axis_size("inner"), lax.axis_size("outer"), rows, width)
    in_hbm = pl.BlockSpec(memory_space=pltpu.HBM)
    kv = lambda parts=1: pltpu.VMEM((2, rows * kv_heads // parts, width), jnp.bfloat16)
    wide = lambda: pltpu.VMEM((rows * heads, width), jnp.float32)
    sems = lambda count: pltpu.SemaphoreType.DMA((count, 2))
    result = pl.pallas_call(
        functools.partial(kernel, dims),
        out_shape=jax.ShapeDtypeStruct((rows * heads, width), jnp.bfloat16),
        in_specs=[in_hbm] * 4,
        out_specs=pl.BlockSpec(memory_space=pl.ANY),
        scratch_shapes=[
            pltpu.VMEM((rows * heads, width), jnp.bfloat16),
            pltpu.VMEM((rows * heads, 2 * width), jnp.bfloat16),
            kv(), kv(), kv(), kv(2),
            pltpu.VMEM((16, LANES), jnp.int32),
            wide(),
            pltpu.VMEM((2 * LANES, 2 * LANES), jnp.bfloat16),
            pltpu.VMEM((2 * width, 2 * LANES), jnp.bfloat16),
            pltpu.VMEM((2 * LANES, 2 * width), jnp.bfloat16),
            wide(), wide(), wide(),
            pltpu.VMEM((rows * heads, width), jnp.bfloat16),
            pltpu.SemaphoreType.DMA((4,)),
            pltpu.SemaphoreType.DMA((2,)),
            sems(8), sems(4), sems(4), sems(4), sems(2), sems(2),
        ],
        compiler_params=pltpu.CompilerParams(
            collective_id=0, has_side_effects=True, vmem_limit_bytes=62 * 1024 * 1024),
    )(
        queries.reshape(rows * heads, width),
        keys.reshape(rows * kv_heads, width),
        values.reshape(rows * kv_heads, width),
        segment_ids.reshape(-1, LANES),
    )
    return result.reshape(rows, heads, width)


def solution(mesh):
    return jax.shard_map(
        shards,
        mesh=mesh,
        in_specs=(
            P(("outer", "inner"), "head", None),
            P(("outer", "inner"), "head", None),
            P(("outer", "inner"), "head", None),
            P(),
        ),
        out_specs=P(("outer", "inner"), "head", None),
        check_vma=False,
    )
```

time: 95.9 us -> 41.6 us (0.43)
  the two profiles are of different devices: /device:TPU:32 before, /device:TPU:184 now
where the time goes in v2:
time: 41.6 us; the launch traced here: 41.4 us
  Pallas kernels  39.2 us (94%)
  local copies, waits for them, and re-layouts  2.26 us (5%)
    pallas_call x1, Pallas kernels, shards(): pl.pallas_call(functools.partial(kernel, dims), out_shape=jax.ShapeDtypeS...  39.2 us
    unnamed x1, local copies, waits for them, and re-layouts  2.26 us

profile of v2, /device:TPU:184, one launch (start us, length us, event | category | flops | bytes accessed | tf_op | source)
XLA Modules:
  0.0 41.4 jit_solution(9574841724661262344)
XLA Ops:
  0.0 39.2 %shard_map.46 = bf16[4096,128]{1,0:T(8,128)(2,1)} custom-call(bf16[4096,128]{1,0:T(8,128)(2,1)} %bitcast.6, bf16[1024,128]{1,0:T(8,128)(2,1)} %bitcast.7, bf16[1024,128]{1,0:T(8,128)(2,1)} %bitcast.8, s32[512,128]{1,0:T(8,128)} %bitcast.9), custom_call_target="tpu_custom_call" | custom-call | tf_op jit(solution)/shard_map/pallas_call | solution.py:306
  39.2 2.3 %copy.6 = bf16[512,8,128]{2,1,0:T(8,128)(2,1)} copy(bf16[512,8,128]{2,1,0:T(8,128)(2,1)} %bitcast.5) | data formatting | bytes 2097152

commit v3 on v2

--- a/solution.py
+++ b/solution.py
@@ -13,8 +13,8 @@
 LANES = 128
 
 
-def kernel(dims, q_hbm, k_hbm, v_hbm, s_hbm, o_hbm, q_in, q_aug, own, near, far, relay, seg, seg_q,
-           perm, k_t, v_cat, top, total, acc, out, in_sem, out_sem,
+def kernel(dims, q_hbm, k_hbm, v_hbm, s_hbm, out, q_in, q_aug, own, near, far, relay, seg, seg_q,
+           perm, k_t, v_cat, top, total, acc, in_sem,
            send_sem, pass_sem, recv_near, recv_far, relay_send, relay_recv):
     inner_size, outer_size, rows, width = dims
     chips_in = inner_size // 2
@@ -93,6 +93,11 @@
     def wait_recv(pair):
         for copy in pair:
             copy.wait_recv()
+
+    def wait_for(target, recv, tile, kv):
+        pltpu.make_async_remote_copy(
+            src_ref=piece(mine[kv], tile), dst_ref=piece(target.at[kv], tile), send_sem=send_sem.at[tile, kv],
+            recv_sem=recv.at[tile, kv], device_id=sibling, device_id_type=MESH).wait_recv()
 
     def wait_send(pair):
         for copy in pair:
@@ -158,16 +163,24 @@
         seg_q[span, :] = jnp.dot(
             picked.astype(jnp.bfloat16), jnp.ones((LANES, LANES), jnp.bfloat16), preferred_element_type=jnp.float32)
 
-    def process(kv_ref, key_block, tiles, first_token, last_token, own_keys=False, init=False):
+    def process(kv_ref, key_block, tiles, first_token, last_token, own_keys=False, init=False, recv=None, last=False):
+        if recv is not None:
+            for tile in tiles:
+                for kv in range(2):
+                    wait_for(kv_ref, recv, tile, kv)
+            recv = None
+
+        def parted(kv, tile):
+            if recv is not None:
+                wait_for(kv_ref, recv, tile, kv)
+            return jnp.dot(
+                perm[...], kv_ref[kv, pl.ds(tile * kv_rows, kv_rows), :], preferred_element_type=jnp.float32)
+
         for part, tile in enumerate(tiles):
             span = pl.ds(part * LANES, LANES)
-            parted = [
-                jnp.dot(perm[...], kv_ref[kv, pl.ds(tile * kv_rows, kv_rows), :], preferred_element_type=jnp.float32)
-                for kv in range(2)]
-            k_t[0:width, span] = parted[0][:LANES].T.astype(jnp.bfloat16)
-            k_t[width:2 * width, span] = parted[0][LANES:].T.astype(jnp.bfloat16)
-            v_cat[span, 0:width] = parted[1][:LANES].astype(jnp.bfloat16)
-            v_cat[span, width:2 * width] = parted[1][LANES:].astype(jnp.bfloat16)
+            both = parted(0, tile)
+            k_t[0:width, span] = both[:LANES].T.astype(jnp.bfloat16)
+            k_t[width:2 * width, span] = both[LANES:].T.astype(jnp.bfloat16)
         ids = jnp.concatenate(
             [seg[pl.ds(key_block * 4 + tile, 1), :] for tile in tiles], axis=1).astype(jnp.float32)
 
@@ -188,24 +201,28 @@
             new_top = jnp.maximum(old_top, peak)
         weights = jnp.exp2((scores - jnp.concatenate([new_top] * len(tiles), axis=1)) * c)
         added = weights[:, :LANES] + weights[:, LANES:]
-        mixed = jnp.dot(weights.astype(jnp.bfloat16), v_cat[...], preferred_element_type=jnp.float32)
+        weights = weights.astype(jnp.bfloat16)
+        for part, tile in enumerate(tiles):
+            both = parted(1, tile)
+            v_cat[pl.ds(part * LANES, LANES), 0:width] = both[:LANES].astype(jnp.bfloat16)
+            v_cat[pl.ds(part * LANES, LANES), width:2 * width] = both[LANES:].astype(jnp.bfloat16)
+        mixed = jnp.dot(weights, v_cat[...], preferred_element_type=jnp.float32)
         line = lax.broadcasted_iota(jnp.int32, (count, width), 0)
         mixed = jnp.where(lax.rem(line, heads) < heads // 2, mixed[:, :width], mixed[:, width:])
-        top[span, :] = new_top
-        if init:
+        if not init:
+            fade = jnp.exp2((old_top - new_top) * c)
+            added = total[span, :] * fade + added
+            mixed = acc[span, :] * fade + mixed
+        if last:
+            out[span, :] = (mixed / jnp.sum(added, axis=1, keepdims=True)).astype(jnp.bfloat16)
+        else:
+            top[span, :] = new_top
             total[span, :] = added
             acc[span, :] = mixed
-        else:
-            fade = jnp.exp2((old_top - new_top) * c)
-            total[span, :] = total[span, :] * fade + added
-            acc[span, :] = acc[span, :] * fade + mixed
-
-    def finish(first_token, last_token, index):
+
+    def finish(first_token, last_token):
         span = pl.ds(first_token * heads, (last_token - first_token) * heads)
         out[span, :] = (acc[span, :] / jnp.sum(total[span, :], axis=1, keepdims=True)).astype(jnp.bfloat16)
-        copy = pltpu.make_async_copy(out.at[span], o_hbm.at[span], out_sem.at[index])
-        copy.start()
-        return copy
 
     half = rows // 2
     process(own, block, (0, 1), 0, rows, own_keys=True, init=True)
@@ -215,22 +232,17 @@
     def _():
         send()
 
-    near_there = has_before | (core == 1)
-    for group, (direct, passed) in enumerate(((1, 3), (0, 2))):
-        @pl.when(has_before & (core == 0))
-        def _():
+    @pl.when(core == 1)
+    def _():
+        for tiles in ((1, 3), (0, 2)):
+            process(near, block - 1, tiles, 0, rows, recv=recv_near if tiles[0] == 0 else None)
+
+    @pl.when(has_before & (core == 0))
+    def _():
+        for direct, passed in ((1, 3), (0, 2)):
             wait_recv(second_by_0(direct))
             start(pass_to_1(direct))
             wait_recv(pass_to_0(passed))
-
-        if group == 1:
-            @pl.when(core == 1)
-            def _():
-                wait_recv(to_core_1(2))
-                wait_recv(to_core_1(0))
-
-        @pl.when(near_there)
-        def _():
             process(near, block - 1, (direct, passed), 0, rows)
 
     @pl.when(has_before & (core == 1))
@@ -238,33 +250,21 @@
         for tile in (3, 2):
             wait_recv(second_by_1(tile))
             start(pass_to_0(tile))
+        process(far, block - 2, (2, 3), 0, rows)
 
     @pl.when(has_before & (core == 0))
     def _():
-        wait_recv(first_by_1(3))
-        wait_recv(first_by_0(2))
+        process(far, block - 2, (2, 3), 0, rows, recv=recv_far)
+
+    finish(half, rows)
 
     @pl.when(has_before)
     def _():
-        process(far, block - 2, (2, 3), 0, rows)
-
-    late = finish(half, rows, 1)
-
-    @pl.when(has_before & (core == 1))
-    def _():
-        wait_recv(pass_to_1(1))
-        wait_recv(pass_to_1(0))
-
-    @pl.when(has_before & (core == 0))
-    def _():
-        wait_recv(first_by_1(1))
-        wait_recv(first_by_0(0))
-
-    @pl.when(has_before)
-    def _():
-        process(far, block - 2, (0, 1), 0, half)
-
-    soon = finish(0, half, 0)
+        process(far, block - 2, (0, 1), 0, half, recv=recv_far, last=True)
+
+    @pl.when(jnp.logical_not(has_before))
+    def _():
+        finish(0, half)
 
     @pl.when(has_after & (core == 1))
     def _():
@@ -290,9 +290,6 @@
     def _():
         for pair in (pass_to_1(1), pass_to_1(0)):
             wait_send(pair)
-
-    late.wait()
-    soon.wait()
 
 
 def shards(queries, keys, values, segment_ids):
@@ -305,9 +302,9 @@
     sems = lambda count: pltpu.SemaphoreType.DMA((count, 2))
     result = pl.pallas_call(
         functools.partial(kernel, dims),
-        out_shape=jax.ShapeDtypeStruct((rows * heads, width), jnp.bfloat16),
+        out_shape=pltpu.VMEM((rows * heads, width), jnp.bfloat16),
         in_specs=[in_hbm] * 4,
-        out_specs=pl.BlockSpec(memory_space=pl.ANY),
+        out_specs=pl.BlockSpec(memory_space=pltpu.VMEM),
         scratch_shapes=[
             pltpu.VMEM((rows * heads, width), jnp.bfloat16),
             pltpu.VMEM((rows * heads, 2 * width), jnp.bfloat16),
@@ -318,19 +315,17 @@
             pltpu.VMEM((2 * width, 2 * LANES), jnp.bfloat16),
             pltpu.VMEM((2 * LANES, 2 * width), jnp.bfloat16),
             wide(), wide(), wide(),
-            pltpu.VMEM((rows * heads, width), jnp.bfloat16),
             pltpu.SemaphoreType.DMA((4,)),
-            pltpu.SemaphoreType.DMA((2,)),
             sems(8), sems(4), sems(4), sems(4), sems(2), sems(2),
         ],
         compiler_params=pltpu.CompilerParams(
-            collective_id=0, has_side_effects=True, vmem_limit_bytes=62 * 1024 * 1024),
-    )(
+            collective_id=0, has_side_effects=True, vmem_limit_bytes=48 * 1024 * 1024),
+    )(*[pltpu.with_memory_space_constraint(operand, pltpu.HBM) for operand in (
         queries.reshape(rows * heads, width),
         keys.reshape(rows * kv_heads, width),
         values.reshape(rows * kv_heads, width),
         segment_ids.reshape(-1, LANES),
-    )
+    )])
     return result.reshape(rows, heads, width)
 
 

time: 41.6 us -> 39.3 us (0.945)
  the two profiles are of different devices: /device:TPU:184 before, /device:TPU:176 now
where the time goes in v3:
time: 39.3 us; the launch traced here: 39.2 us
  Pallas kernels  38.2 us (97%)
  local copies, waits for them, and re-layouts  0.97 us (2%)
    pallas_call x1, Pallas kernels, shards(): pl.pallas_call(functools.partial(kernel, dims), out_shape=pltpu.VMEM((row...  38.2 us
    unnamed x1, local copies, waits for them, and re-layouts  0.97 us

profile of v3, /device:TPU:176, one launch (start us, length us, event | category | flops | bytes accessed | tf_op | source)
XLA Modules:
  0.0 39.2 jit_solution(9726511274286631081)
XLA Ops:
  0.0 38.2 %shard_map.46 = bf16[4096,128]{1,0:T(8,128)(2,1)S(1)} custom-call(bf16[4096,128]{1,0:T(8,128)(2,1)} %bitcast.6, bf16[1024,128]{1,0:T(8,128)(2,1)} %bitcast.7, bf16[1024,128]{1,0:T(8,128)(2,1)} %bitcast.8, s32[512,128]{1,0:T(8,128)} %bitcast.9), custom_call_target="tpu_custom_call" | custom-call | tf_op jit(solution)/shard_map/pallas_call | solution.py:303
  38.2 1.0 %copy.6 = bf16[512,8,128]{2,1,0:T(8,128)(2,1)} copy(bf16[512,8,128]{2,1,0:T(8,128)(2,1)S(1)} %bitcast.5) | data formatting | bytes 2097152

commit v4 on v3

v4 whole, which is shorter than its diff:
```python
import functools

import jax
import jax.numpy as jnp
from jax import lax
from jax.experimental import pallas as pl
from jax.experimental.pallas import tpu as pltpu
from jax.sharding import PartitionSpec as P

MESH = pl.DeviceIdType.MESH
BIG = -1e30
LOG2E = 1.4426950408889634
LANES = 128


def kernel(dims, q_hbm, k_hbm, v_hbm, s_hbm, out, q_in, q_aug, own, near, far, relay, seg, seg_q,
           perm, k_t, v_cat, top, total, acc, in_sem,
           send_sem, pass_sem, recv_near, recv_far, relay_send, relay_recv):
    inner_size, outer_size, rows, width = dims
    chips_in = inner_size // 2
    outer, inner, head = lax.axis_index("outer"), lax.axis_index("inner"), lax.axis_index("head")
    chip, core = outer * chips_in + inner // 2, lax.rem(inner, 2)
    early = lax.rem(chip, 2) == 0
    has_before, has_after = chip > 0, chip < outer_size * chips_in - 1
    heads = q_in.shape[0] // rows
    kv_rows = own.shape[1] // rows * LANES
    c = (width ** -0.5) * LOG2E

    def device(index, which):
        return (index // chips_in, lax.rem(index, chips_in) * 2 + which, head)

    sibling = (outer, inner + 1 - 2 * core, head)

    barrier = pltpu.get_barrier_semaphore()
    pl.semaphore_signal(barrier, inc=1, device_id=sibling, device_id_type=MESH)

    @pl.when(has_before)
    def _():
        pl.semaphore_signal(barrier, inc=1, device_id=device(chip - 1, 1), device_id_type=MESH)

    @pl.when(has_before & (core == 0))
    def _():
        pl.semaphore_signal(barrier, inc=1, device_id=device(chip - 1, 0), device_id_type=MESH)

    loads = [
        pltpu.make_async_copy(k_hbm, own.at[0], in_sem.at[0]),
        pltpu.make_async_copy(v_hbm, own.at[1], in_sem.at[1]),
        pltpu.make_async_copy(q_hbm, q_in, in_sem.at[2]),
        pltpu.make_async_copy(s_hbm.at[pl.ds(pl.multiple_of(jnp.maximum(chip - 1, 0) * 8, 8), 16)], seg, in_sem.at[3]),
    ]

    def piece(ref, tile):
        return ref.at[pl.ds(tile * kv_rows, kv_rows)]

    def copy_of(source, target, tile, kv, send, recv, to, slot=0):
        return pltpu.make_async_remote_copy(
            src_ref=piece(source, tile), dst_ref=piece(target.at[kv], tile),
            send_sem=send.at[slot + tile, kv], recv_sem=recv.at[tile, kv], device_id=to, device_id_type=MESH)

    def second_keys(tile):
        return copy_of(k_hbm, far, tile, 0, send_sem, recv_far, device(chip + 1, 1))

    def first_keys(tile):
        return copy_of(near.at[0], far, tile, 0, send_sem, recv_far, device(chip + 1, 0), 4)

    def second_values(tile):
        return copy_of(relay, near, tile, 1, send_sem, recv_near, device(chip + 1, 0))

    def first_values(tile):
        return copy_of(v_hbm, far, tile, 1, send_sem, recv_far, device(chip + 1, 0), 4)

    def to_core_1(tile, kv):
        return copy_of((k_hbm, v_hbm)[kv], near, tile, kv, pass_sem, recv_near, sibling)

    def to_relay(tile):
        return pltpu.make_async_remote_copy(
            src_ref=piece(v_hbm, tile), dst_ref=piece(relay, tile), send_sem=relay_send.at[tile],
            recv_sem=relay_recv.at[tile], device_id=sibling, device_id_type=MESH)

    def pass_keys(tile):
        return copy_of(far.at[0], near, tile, 0, pass_sem, recv_near, sibling)

    def pass_values(tile):
        return copy_of(near.at[1], far, tile, 1, pass_sem, recv_far, sibling, 4)

    def wait_near(tile, kv):
        to_core_1(tile, kv).wait_recv()

    def wait_far(tile, kv):
        copy_of((k_hbm, v_hbm)[kv], far, tile, kv, pass_sem, recv_far, sibling).wait_recv()

    order = (3, 2, 1, 0)

    def send():
        pl.semaphore_wait(barrier, 1 + has_after.astype(jnp.int32) * (1 + core))

        @pl.when(core == 1)
        def _():
            @pl.when(has_after)
            def _():
                for tile in order:
                    to_relay(tile).start()
                    second_keys(tile).start()
            for tile in order:
                wait_near(tile, 0)

            @pl.when(has_after)
            def _():
                for tile in order:
                    first_keys(tile).start()

        @pl.when(core == 0)
        def _():
            for kv in range(2):
                for tile in order:
                    to_core_1(tile, kv).start()

            @pl.when(has_after)
            def _():
                for tile in order:
                    to_relay(tile).wait_recv()
                    second_values(tile).start()
                for tile in order:
                    first_values(tile).start()

    for load in loads:
        load.start()

    @pl.when(jnp.logical_not(early))
    def _():
        send()

    at = lax.broadcasted_iota(jnp.int32, perm.shape, 0)
    taken = jnp.where(at < LANES, 2 * at, 2 * at - 2 * LANES + 1)
    perm[...] = (taken == lax.broadcasted_iota(jnp.int32, perm.shape, 1)).astype(jnp.float32).astype(jnp.bfloat16)
    for load in loads:
        load.wait()
    base = jnp.maximum(chip - 1, 0) * 2
    block = chip * 2 + core - base

    shape = (LANES * heads, LANES)
    row = lax.broadcasted_iota(jnp.int32, shape, 0)
    first_half = lax.rem(row, heads) < heads // 2
    for tile in range(rows // LANES):
        span = pl.ds(tile * LANES * heads, LANES * heads)
        q = q_in[span, :].astype(jnp.float32)
        q_aug[span, 0:width] = jnp.where(first_half, q, 0.0).astype(jnp.bfloat16)
        q_aug[span, width:2 * width] = jnp.where(first_half, 0.0, q).astype(jnp.bfloat16)
        ids = seg[pl.ds(block * 4 + tile, 1), :].astype(jnp.float32)
        picked = jnp.where(row // heads == lax.broadcasted_iota(jnp.int32, shape, 1), ids, 0.0)
        seg_q[span, :] = jnp.dot(
            picked.astype(jnp.bfloat16), jnp.ones((LANES, LANES), jnp.bfloat16), preferred_element_type=jnp.float32)

    def process(kv_ref, key_block, tiles, spans, own_keys=False, init=False, last=False):
        for part, tile in enumerate(tiles):
            span = pl.ds(part * LANES, LANES)
            parted = [
                jnp.dot(perm[...], kv_ref[kv, pl.ds(tile * kv_rows, kv_rows), :], preferred_element_type=jnp.float32)
                for kv in range(2)]
            k_t[0:width, span] = parted[0][:LANES].T.astype(jnp.bfloat16)
            k_t[width:2 * width, span] = parted[0][LANES:].T.astype(jnp.bfloat16)
            v_cat[span, 0:width] = parted[1][:LANES].astype(jnp.bfloat16)
            v_cat[span, width:2 * width] = parted[1][LANES:].astype(jnp.bfloat16)
        for first_token, last_token, low in spans:
            step(key_block, tiles[low:], slice(low * LANES, len(tiles) * LANES), first_token, last_token,
                 own_keys, init, last)

    def step(key_block, tiles, reach, first_token, last_token, own_keys, init, last):
        ids = jnp.concatenate(
            [seg[pl.ds(key_block * 4 + tile, 1), :] for tile in tiles], axis=1).astype(jnp.float32)
        begin, count = first_token * heads, (last_token - first_token) * heads
        span = pl.ds(begin, count)
        scores = jnp.dot(q_aug[span, :], k_t[:, reach], preferred_element_type=jnp.float32)
        allowed = jnp.concatenate([seg_q[span, :]] * len(tiles), axis=1) == ids
        if own_keys:
            line = lax.broadcasted_iota(jnp.int32, scores.shape, 0)
            key = lax.broadcasted_iota(jnp.int32, scores.shape, 1)
            allowed = allowed & (line - heads * key >= heads * tiles[0] * LANES - begin)
        scores = jnp.where(allowed, scores, BIG)
        peak = jnp.max(scores, axis=1, keepdims=True)
        if init:
            new_top = jnp.broadcast_to(peak, (count, LANES))
        else:
            old_top = top[span, :]
            new_top = jnp.maximum(old_top, peak)
        weights = jnp.exp2((scores - jnp.concatenate([new_top] * len(tiles), axis=1)) * c)
        added = weights if len(tiles) == 1 else weights[:, :LANES] + weights[:, LANES:]
        mixed = jnp.dot(weights.astype(jnp.bfloat16), v_cat[reach, :], preferred_element_type=jnp.float32)
        line = lax.broadcasted_iota(jnp.int32, (count, width), 0)
        mixed = jnp.where(lax.rem(line, heads) < heads // 2, mixed[:, :width], mixed[:, width:])
        if not init:
            fade = jnp.exp2((old_top - new_top) * c)
            added = total[span, :] * fade + added
            mixed = acc[span, :] * fade + mixed
        if last:
            out[span, :] = (mixed / jnp.sum(added, axis=1, keepdims=True)).astype(jnp.bfloat16)
        else:
            top[span, :] = new_top
            total[span, :] = added
            acc[span, :] = mixed

    def finish(first_token, last_token):
        span = pl.ds(first_token * heads, (last_token - first_token) * heads)
        out[span, :] = (acc[span, :] / jnp.sum(total[span, :], axis=1, keepdims=True)).astype(jnp.bfloat16)

    half = rows // 2
    process(own, block, (0, 1), [(0, rows, 0)], own_keys=True, init=True)
    process(own, block, (2, 3), [(half, rows, 0)], own_keys=True)

    @pl.when(early)
    def _():
        send()

    for tiles in ((2, 3), (0, 1)):
        @pl.when(core == 1)
        def _():
            for tile in tiles:
                wait_near(tile, 1)

        @pl.when(has_before & (core == 0))
        def _():
            for tile in reversed(tiles):
                wait_near(tile, 1)
                pass_values(tile).start()
            for tile in tiles:
                wait_near(tile, 0)

        @pl.when(has_before | (core == 1))
        def _():
            process(near, block - 1, tiles, [(0, rows, 0)])

    @pl.when(has_before & (core == 1))
    def _():
        for tile in order:
            wait_far(tile, 0)
            pass_keys(tile).start()

    def far_step(tiles, spans, last=False):
        @pl.when(has_before & (core == 0))
        def _():
            for tile in tiles:
                wait_far(tile, 0)

        @pl.when(has_before)
        def _():
            for tile in tiles:
                wait_far(tile, 1)
            process(far, block - 2, tiles, spans, last=last)

    far_step((2, 3), [(0, rows - LANES, 0), (rows - LANES, rows, 1)])
    finish(half, rows)
    @pl.when(core == 0)
    def _():
        for tile in order:
            for kv in range(2):
                to_core_1(tile, kv).wait_send()

    @pl.when(has_before & (core == 0))
    def _():
        for tile in order:
            pass_values(tile).wait_send()

    far_step((0, 1), [(0, LANES, 0), (LANES, half, 1)], last=True)

    @pl.when(jnp.logical_not(has_before))
    def _():
        finish(0, half)

    @pl.when(has_after & (core == 1))
    def _():
        for tile in order:
            to_relay(tile).wait_send()
            second_keys(tile).wait_send()
            first_keys(tile).wait_send()

    @pl.when(has_after & (core == 0))
    def _():
        for tile in order:
            second_values(tile).wait_send()
            first_values(tile).wait_send()

    @pl.when(has_before & (core == 1))
    def _():
        for tile in order:
            pass_keys(tile).wait_send()


def shards(queries, keys, values, segment_ids):
    rows, heads, width = queries.shape
    kv_heads = keys.shape[1]
    dims = (lax.axis_size("inner"), lax.axis_size("outer"), rows, width)
    in_hbm = pl.BlockSpec(memory_space=pltpu.HBM)
    kv = lambda: pltpu.VMEM((2, rows * kv_heads, width), jnp.bfloat16)
    wide = lambda: pltpu.VMEM((rows * heads, width), jnp.float32)
    sems = lambda count: pltpu.SemaphoreType.DMA((count, 2))
    result = pl.pallas_call(
        functools.partial(kernel, dims),
        out_shape=pltpu.VMEM((rows * heads, width), jnp.bfloat16),
        in_specs=[in_hbm] * 4,
        out_specs=pl.BlockSpec(memory_space=pltpu.VMEM),
        scratch_shapes=[
            pltpu.VMEM((rows * heads, width), jnp.bfloat16),
            pltpu.VMEM((rows * heads, 2 * width), jnp.bfloat16),
            kv(), kv(), kv(),
            pltpu.VMEM((rows * kv_heads, width), jnp.bfloat16),
            pltpu.VMEM((16, LANES), jnp.int32),
            wide(),
            pltpu.VMEM((2 * LANES, 2 * LANES), jnp.bfloat16),
            pltpu.VMEM((2 * width, 2 * LANES), jnp.bfloat16),
            pltpu.VMEM((2 * LANES, 2 * width), jnp.bfloat16),
            wide(), wide(), wide(),
            pltpu.SemaphoreType.DMA((4,)),
            sems(8), sems(8), sems(4), sems(4),
            pltpu.SemaphoreType.DMA((4,)),
            pltpu.SemaphoreType.DMA((4,)),
        ],
        compiler_params=pltpu.CompilerParams(
            collective_id=0, has_side_effects=True, vmem_limit_bytes=48 * 1024 * 1024),
    )(*[pltpu.with_memory_space_constraint(operand, pltpu.HBM) for operand in (
        queries.reshape(rows * heads, width),
        keys.reshape(rows * kv_heads, width),
        values.reshape(rows * kv_heads, width),
        segment_ids.reshape(-1, LANES),
    )])
    return result.reshape(rows, heads, width)


def solution(mesh):
    return jax.shard_map(
        shards,
        mesh=mesh,
        in_specs=(
            P(("outer", "inner"), "head", None),
            P(("outer", "inner"), "head", None),
            P(("outer", "inner"), "head", None),
            P(),
        ),
        out_specs=P(("outer", "inner"), "head", None),
        check_vma=False,
    )
```

time: 39.3 us -> 39 us (level)
  the two profiles are of different devices: /device:TPU:176 before, /device:TPU:168 now
where the time goes in v4:
time: 39 us; the launch traced here: 38.9 us
  Pallas kernels  37.9 us (97%)
  local copies, waits for them, and re-layouts  0.97 us (2%)
    pallas_call x1, Pallas kernels, shards(): pl.pallas_call(functools.partial(kernel, dims), out_shape=pltpu.VMEM((row...  37.9 us
    unnamed x1, local copies, waits for them, and re-layouts  0.97 us

profile of v4, /device:TPU:168, one launch (start us, length us, event | category | flops | bytes accessed | tf_op | source)
XLA Modules:
  0.0 38.9 jit_solution(4850833067678089678)
XLA Ops:
  0.0 37.9 %shard_map.46 = bf16[4096,128]{1,0:T(8,128)(2,1)S(1)} custom-call(bf16[4096,128]{1,0:T(8,128)(2,1)} %bitcast.6, bf16[1024,128]{1,0:T(8,128)(2,1)} %bitcast.7, bf16[1024,128]{1,0:T(8,128)(2,1)} %bitcast.8, s32[512,128]{1,0:T(8,128)} %bitcast.9), custom_call_target="tpu_custom_call" | custom-call | tf_op jit(solution)/shard_map/pallas_call | solution.py:296
  37.9 1.0 %copy.6 = bf16[512,8,128]{2,1,0:T(8,128)(2,1)} copy(bf16[512,8,128]{2,1,0:T(8,128)(2,1)S(1)} %bitcast.5) | data formatting | bytes 2097152

commit v5 on v4

--- a/solution.py
+++ b/solution.py
@@ -151,7 +151,7 @@
         seg_q[span, :] = jnp.dot(
             picked.astype(jnp.bfloat16), jnp.ones((LANES, LANES), jnp.bfloat16), preferred_element_type=jnp.float32)
 
-    def process(kv_ref, key_block, tiles, spans, own_keys=False, init=False, last=False):
+    def process(kv_ref, key_block, tiles, spans, own_keys=False, init=False, last=1 << 30):
         for part, tile in enumerate(tiles):
             span = pl.ds(part * LANES, LANES)
             parted = [
@@ -163,7 +163,7 @@
             v_cat[span, width:2 * width] = parted[1][LANES:].astype(jnp.bfloat16)
         for first_token, last_token, low in spans:
             step(key_block, tiles[low:], slice(low * LANES, len(tiles) * LANES), first_token, last_token,
-                 own_keys, init, last)
+                 own_keys, init, first_token >= last)
 
     def step(key_block, tiles, reach, first_token, last_token, own_keys, init, last):
         ids = jnp.concatenate(
@@ -235,7 +235,7 @@
             wait_far(tile, 0)
             pass_keys(tile).start()
 
-    def far_step(tiles, spans, last=False):
+    def far_step(tiles, spans, last):
         @pl.when(has_before & (core == 0))
         def _():
             for tile in tiles:
@@ -247,8 +247,7 @@
                 wait_far(tile, 1)
             process(far, block - 2, tiles, spans, last=last)
 
-    far_step((2, 3), [(0, rows - LANES, 0), (rows - LANES, rows, 1)])
-    finish(half, rows)
+    far_step((2, 3), [(0, half, 0), (half, rows - LANES, 0), (rows - LANES, rows, 1)], last=half)
     @pl.when(core == 0)
     def _():
         for tile in order:
@@ -260,11 +259,11 @@
         for tile in order:
             pass_values(tile).wait_send()
 
-    far_step((0, 1), [(0, LANES, 0), (LANES, half, 1)], last=True)
+    far_step((0, 1), [(0, LANES, 0), (LANES, half, 1)], last=0)
 
     @pl.when(jnp.logical_not(has_before))
     def _():
-        finish(0, half)
+        finish(0, rows)
 
     @pl.when(has_after & (core == 1))
     def _():

time: 39 us -> 38.7 us (level)
  the two profiles are of different devices: /device:TPU:168 before, /device:TPU:176 now
where the time goes in v5:
time: 38.7 us; the launch traced here: 38.6 us
  Pallas kernels  37.6 us (97%)
  local copies, waits for them, and re-layouts  0.97 us (3%)
    pallas_call x1, Pallas kernels, shards(): pl.pallas_call(functools.partial(kernel, dims), out_shape=pltpu.VMEM((row...  37.6 us
    unnamed x1, local copies, waits for them, and re-layouts  0.97 us

profile of v5, /device:TPU:176, one launch (start us, length us, event | category | flops | bytes accessed | tf_op | source)
XLA Modules:
  0.0 38.6 jit_solution(9933621563409019253)
XLA Ops:
  0.0 37.6 %shard_map.46 = bf16[4096,128]{1,0:T(8,128)(2,1)S(1)} custom-call(bf16[4096,128]{1,0:T(8,128)(2,1)} %bitcast.6, bf16[1024,128]{1,0:T(8,128)(2,1)} %bitcast.7, bf16[1024,128]{1,0:T(8,128)(2,1)} %bitcast.8, s32[512,128]{1,0:T(8,128)} %bitcast.9), custom_call_target="tpu_custom_call" | custom-call | tf_op jit(solution)/shard_map/pallas_call | solution.py:295
  37.6 1.0 %copy.6 = bf16[512,8,128]{2,1,0:T(8,128)(2,1)} copy(bf16[512,8,128]{2,1,0:T(8,128)(2,1)S(1)} %bitcast.5) | data formatting | bytes 2097152
